TPU v7x, 32 devices: a whole 2x2x4 slice. The times are simulated.
32 devices in a mesh: rows: 8 (over y, x, core), cols: 4 (over z).
Axes of the slice: x: 2, y: 2, z: 4, core: 2. Of those that a mesh axis runs over, the one named last changes fastest.
Arguments:
- basis: float32 [512, 4096], P(None, ('cols', 'rows')), may hold values from -6 to 6
- tile_counts: int32 [1024, 128, 128], P(('rows', 'cols')), may hold values from 0 to 63
- tile_rows: int32 [1024], P(('rows', 'cols')), may hold values from 0 to 3
- tile_cols: int32 [1024], P(('rows', 'cols')), may hold values from 0 to 7
- tile_live: int32 [32], P(('rows', 'cols')), may hold values from 8 to 32, as said below
- marginals: int32 [4096], replicated, may hold values from 1 to 983040, as said below
Outputs:
- subspace: float32 [512, 4096], P(None, ('cols', 'rows'))
Inputs may be any that keep to these rules, and one draw needn't show every extreme that they name: `tile_live`: every list has at least a quarter of its 32 slots live; some list has all 32 live. `marginals`: A small multiplier times a power of four.
All inputs are finite; a program needn't handle non-finite values.
Results may differ from a plain program's by a relative error of at most 0.012.
The roundings to bfloat16 on the way count: a program that leaves them out, or rounds other values in their place, can miss the bound.
Values may be sent and summed in bfloat16 or wider, within the bound.
A program may use at most 128 MiB of HBM per device.

v0:
```python
import functools

import jax
import jax.numpy as jnp
from jax import lax
from jax.experimental import pallas as pl
from jax.experimental.pallas import tpu as pltpu
from jax.sharding import PartitionSpec as P

ITERS = 2
HIGHEST = lax.Precision.HIGHEST
MESH = pl.DeviceIdType.MESH
VMEM = pl.BlockSpec(memory_space=pltpu.VMEM)
SMEM = pl.BlockSpec(memory_space=pltpu.SMEM)
BLOCK = 128
PANEL = 16


def dot_nt(left, right, precision=HIGHEST):
    return lax.dot_general(
        left, right, (((1,), (1,)), ((), ())), precision=precision, preferred_element_type=jnp.float32
    )


def dot_tn(left, right):
    return lax.dot_general(
        left, right, (((0,), (0,)), ((), ())), precision=HIGHEST, preferred_element_type=jnp.float32
    )


def dot_nn(left, right):
    return jnp.dot(left, right, precision=HIGHEST, preferred_element_type=jnp.float32)


def matrix_kernel(rows_ref, cols_ref, live_ref, total_ref, counts_ref, row_logs_ref, col_logs_ref, high_ref, low_ref, dense):
    tile = counts_ref.shape[1]
    log_total = total_ref[0]
    dense[...] = jnp.zeros_like(dense)

    def add_tile(slot, carry):
        row = pl.multiple_of(rows_ref[slot] * tile, tile)
        col = pl.multiple_of(cols_ref[slot] * tile, tile)
        counts = counts_ref[slot]
        ratio = (
            jnp.log(jnp.maximum(counts.astype(jnp.float32), 1.0))
            + log_total
            - row_logs_ref[pl.ds(row, tile), :]
            - col_logs_ref[:, pl.ds(col, tile)]
        )
        value = jnp.where(counts > 0, jnp.maximum(ratio, 0.0), 0.0)
        value = value.astype(jnp.bfloat16).astype(jnp.float32)
        dense[pl.ds(row, tile), pl.ds(col, tile)] += value
        return carry

    lax.fori_loop(0, live_ref[0], add_tile, 0)

    def split(block, carry):
        here = pl.ds(pl.multiple_of(block * tile, tile), tile)
        whole = dense[here, :]
        high = whole.astype(jnp.bfloat16)
        high_ref[here, :] = high
        low_ref[here, :] = (whole - high.astype(jnp.float32)).astype(jnp.bfloat16)
        return carry

    lax.fori_loop(0, dense.shape[0] // tile, split, 0)


def build_matrix(tile_rows, tile_cols, tile_live, log_total, tile_counts, row_logs, col_logs):
    shape = (row_logs.shape[0], col_logs.shape[1])
    return pl.pallas_call(
        matrix_kernel,
        out_shape=[jax.ShapeDtypeStruct(shape, jnp.bfloat16)] * 2,
        in_specs=[SMEM] * 4 + [VMEM] * 3,
        out_specs=[VMEM] * 2,
        scratch_shapes=[pltpu.VMEM(shape, jnp.float32)],
        compiler_params=pltpu.CompilerParams(vmem_limit_bytes=56 * 2**20),
    )(tile_rows, tile_cols, tile_live, log_total, tile_counts, row_logs, col_logs)


def block_pairs(width):
    count = width // BLOCK
    return [(i, j) for i in range(count) for j in range(i, count)]


def iterate_kernel(chips, depth, cur_ref, high_ref, low_ref, out_ref, share, work, small, *rounds):
    row = lax.axis_index("rows")
    level = lax.axis_index("cols")
    chip = row // 2
    core = row % 2
    sibling = {"rows": chip * 2 + (1 - core), "cols": level}
    plane = [{"rows": lax.rem(chip + k, chips) * 2 + core, "cols": level} for k in range(1, chips)]
    column = [{"rows": row, "cols": lax.rem(level + k, depth)} for k in range(1, depth)]
    peers = [sibling] + plane + column
    above, below = column[0], column[depth - 2]
    barrier = pltpu.get_barrier_semaphore()
    for peer in peers:
        pl.semaphore_signal(barrier, inc=1, device_id=peer, device_id_type=MESH)
    width, terms = cur_ref.shape
    chunk = BLOCK
    chunks = width // chunk
    others = chips - 1
    last = depth - 1
    pair = 2 * terms
    pairs = block_pairs(width)
    lanes = pl.ds(pl.multiple_of(core * terms, terms), terms)

    def rows_at(start, size):
        return pl.ds(pl.multiple_of(start, 8), size)

    def block_at(index):
        return pl.ds(pl.multiple_of(index * BLOCK, BLOCK), BLOCK)

    def remote(source, target, sent, received, peer):
        return pltpu.make_async_remote_copy(
            src_ref=source,
            dst_ref=target,
            send_sem=sent,
            recv_sem=received,
            device_id=peer,
            device_id_type=MESH,
        )

    def send(source, target, sends, receives, index, peer):
        copy = remote(source, target, sends.at[index], receives.at[index], peer)
        copy.start()
        return copy

    def each(count, step):
        def body(index, carry):
            step(index)
            return carry

        lax.fori_loop(0, count, body, 0)

    def make_round(
        basis, part, inbox, relay, mine, core_in, plane_in, z_in, gram,
        near_send, near_recv, far_send, far_recv, pass_send, pass_recv, sum_send, sum_recv, relay_send, relay_recv,
        core_send, core_recv, plane_send, plane_recv, z_send, z_recv,
    ):
        def near_copy(q):
            own = basis.at[chip, block_at(q), lanes]
            return remote(own, own, near_send.at[q], near_recv.at[q], sibling)

        def far_copy(q, k):
            own = basis.at[chip, block_at(q), lanes]
            index = q * others + k
            return remote(own, own, far_send.at[index], far_recv.at[index], plane[k])

        def pass_copy(q, k):
            there = basis.at[lax.rem(chip + others - k, chips), block_at(q), lanes]
            index = q * others + k
            return remote(there, there, pass_send.at[index], pass_recv.at[index], sibling)

        def direct_copy(q, k):
            return remote(part.at[q, lax.rem(level + k, depth)], inbox.at[q, level], sum_send.at[q * depth + k], sum_recv.at[q * depth + level], column[k - 1])

        def relay_copy(q, target, peer):
            return remote(part.at[q, target], relay.at[q], relay_send.at[q], relay_recv.at[q], peer)

        def gather(q, vectors):
            basis[chip, block_at(q), lanes] = vectors.astype(jnp.bfloat16)
            for k in range(others):
                far_copy(q, k).start()
            near_copy(q).start()

        def multiply(q):
            for k in range(others):
                far_copy(q, k).wait_recv()
                pass_copy(q, k).start()
            near_copy(q).wait_recv()
            total = None
            for k in range(chips):
                if k:
                    pass_copy(q, k - 1).wait_recv()
                source = lax.rem(chip + chips - k, chips)
                columns = pl.ds(pl.multiple_of(source * pair, pair), pair)
                vectors = basis[source, block_at(q), :]
                product = dot_nt(vectors, high_ref[:, columns], None) + dot_nt(vectors, low_ref[:, columns], None)
                total = product if total is None else total + product
            for l in range(depth):
                part[q, l] = total[:, l * terms : (l + 1) * terms]

            @pl.when(level == 0)
            def _():
                relay_copy(q, last, above).start()

            @pl.when(level == last)
            def _():
                relay_copy(q, 0, below).start()

            for k in range(1, depth):
                target = lax.rem(level + k, depth)
                waits = ((level <= 1) & (target == last)) | ((level >= last - 1) & (target == 0))

                @pl.when(jnp.logical_not(waits))
                def _():
                    direct_copy(q, k).start()

        def pass_relay(q):
            @pl.when(level == 1)
            def _():
                relay_copy(q, last, above).wait_recv()
                part[q, last] += relay[q]
                direct_copy(q, last - 1).start()

            @pl.when(level == last - 1)
            def _():
                relay_copy(q, 0, below).wait_recv()
                part[q, 0] += relay[q]
                direct_copy(q, 2).start()

        def collect(q):
            share[block_at(q), :] = part[q, level]
            for u in range(depth):
                absent = (level == u) | ((level == last) & (u == 0)) | ((level == 0) & (u == last))

                @pl.when(jnp.logical_not(absent))
                def _():
                    remote(part.at[q, u], inbox.at[q, u], sum_send.at[q * depth], sum_recv.at[q * depth + u], above).wait_recv()
                    share[block_at(q), :] += inbox[q, u]

        def wait_sent(q):
            near_copy(q).wait_send()
            for k in range(others):
                far_copy(q, k).wait_send()
                pass_copy(q, k).wait_send()
            for k in range(1, depth):
                by_relay = ((level == 0) & (k == last)) | ((level == last) & (k == 1))

                @pl.when(jnp.logical_not(by_relay))
                def _():
                    direct_copy(q, k).wait_send()

            @pl.when(level == 0)
            def _():
                relay_copy(q, last, above).wait_send()

            @pl.when(level == last)
            def _():
                relay_copy(q, 0, below).wait_send()

        def reduce_gram():
            total = mine.shape[0]
            half = total // 2
            piece = half // chips
            portion = piece // depth
            for index, (i, j) in enumerate(pairs):
                mine[index * BLOCK : (index + 1) * BLOCK, :] = dot_nt(
                    share[i * BLOCK : (i + 1) * BLOCK, :], share[j * BLOCK : (j + 1) * BLOCK, :]
                )
            used = len(pairs) * BLOCK
            if used < total:
                mine[used:, :] = jnp.zeros((total - used, BLOCK), jnp.float32)

            half_start = core * half
            first = send(mine.at[rows_at((1 - core) * half, half)], core_in, core_send, core_recv, 0, sibling)
            each(chunks, wait_sent)
            first.wait()
            mine[rows_at(half_start, half), :] += core_in[...]

            piece_start = half_start + chip * piece
            copies = [
                send(mine.at[rows_at(half_start + lax.rem(chip + k, chips) * piece, piece)], plane_in.at[k - 1], plane_send, plane_recv, k - 1, plane[k - 1])
                for k in range(1, chips)
            ]
            for copy in copies:
                copy.wait()
            summed = mine[rows_at(piece_start, piece), :]
            for k in range(1, chips):
                summed += plane_in[k - 1]
            mine[rows_at(piece_start, piece), :] = summed

            part_start = piece_start + level * portion
            copies = [
                send(mine.at[rows_at(piece_start + lax.rem(level + k, depth) * portion, portion)], z_in.at[k - 1], z_send, z_recv, k - 1, column[k - 1])
                for k in range(1, depth)
            ]
            for copy in copies:
                copy.wait()
            summed = mine[rows_at(part_start, portion), :]
            for k in range(1, depth):
                summed += z_in[k - 1]
            gram[rows_at(part_start, portion), :] = summed

            here = gram.at[rows_at(part_start, portion)]
            copies = [
                send(here, here, z_send, z_recv, depth - 2 + k, column[k - 1]) for k in range(1, depth)
            ]
            for copy in copies:
                copy.wait()
            here = gram.at[rows_at(piece_start, piece)]
            copies = [
                send(here, here, plane_send, plane_recv, chips - 2 + k, plane[k - 1]) for k in range(1, chips)
            ]
            for copy in copies:
                copy.wait()
            here = gram.at[rows_at(half_start, half)]
            send(here, here, core_send, core_recv, 1, sibling).wait()
            for index, (i, j) in enumerate(pairs):
                work[i * BLOCK : (i + 1) * BLOCK, j * BLOCK : (j + 1) * BLOCK] = gram[index * BLOCK : (index + 1) * BLOCK, :]
            work[:, width:] = share[...]

        return gather, multiply, pass_relay, collect, reduce_gram

    sublane = lax.broadcasted_iota(jnp.int32, (PANEL, BLOCK), 0)
    unit = (
        lax.broadcasted_iota(jnp.int32, (BLOCK, BLOCK), 0) == lax.broadcasted_iota(jnp.int32, (BLOCK, BLOCK), 1)
    ).astype(jnp.float32)

    def eliminate(b):
        here = block_at(b)
        small[:, :BLOCK] = work[here, here]
        small[:, BLOCK:] = unit
        for start in range(0, BLOCK, PANEL):
            left = small[start : start + PANEL, :BLOCK]
            right = small[start : start + PANEL, BLOCK:]
            spread = [
                jnp.broadcast_to(left[:, start + k : start + k + 1], (PANEL, BLOCK)) for k in range(PANEL)
            ]
            for i in range(PANEL):
                inverse = lax.rsqrt(spread[i][i : i + 1, :])
                left_row = left[i : i + 1, :] * inverse
                right_row = right[i : i + 1, :] * inverse
                scale = jnp.where(sublane > i, spread[i] * inverse, 0.0)
                left = jnp.where(sublane == i, left_row, left - scale * left_row)
                right = jnp.where(sublane == i, right_row, right - scale * right_row)
                for k in range(i + 1, PANEL):
                    spread[k] = spread[k] - scale * (spread[k][i : i + 1, :] * inverse)
            small[start : start + PANEL, :BLOCK] = left
            small[start : start + PANEL, BLOCK:] = right
            rest = start + PANEL
            if rest < BLOCK:
                both = small[start : start + PANEL, :]
                small[rest:, :] -= dot_tn(left, both)[rest:, :]
        solved = dot_nn(small[:, BLOCK:], work[here, :])
        work[here, :] = solved
        return solved[:, width:]

    def update(b):
        def body(i, carry):
            work[block_at(i), :] -= dot_tn(work[block_at(b), block_at(i)], work[block_at(b), :])
            return carry

        lax.fori_loop(b + 1, chunks, body, 0)

    per = len(rounds) // ITERS
    parts = [make_round(*rounds[it * per : (it + 1) * per]) for it in range(ITERS)]
    pl.semaphore_wait(barrier, len(peers))
    gather, multiply = parts[0][:2]
    each(chunks, lambda q: gather(q, cur_ref[block_at(q), :]))
    each(chunks, multiply)
    for it in range(ITERS):
        pass_relay, collect, reduce_gram = parts[it][2:]
        each(chunks, pass_relay)
        each(chunks, collect)
        reduce_gram()
        if it + 1 < ITERS:
            gather, multiply = parts[it + 1][:2]

            def step(b):
                gather(b, eliminate(b))
                update(b)

                @pl.when(b > 0)
                def _():
                    multiply(b - 1)

            each(chunks, step)
            multiply(chunks - 1)
        else:

            def final(b):
                out_ref[block_at(b), :] = eliminate(b)
                update(b)

            each(chunks, final)


def iterate(current, high, low):
    chips = lax.axis_size("rows") // 2
    depth = lax.axis_size("cols")
    width, terms = current.shape
    chunks = width // BLOCK
    unit = 8 * 2 * chips * depth
    used = len(block_pairs(width)) * BLOCK
    total = -(-used // unit) * unit
    half = total // 2
    piece = half // chips
    portion = piece // depth

    def floats(*shape):
        return pltpu.VMEM(shape, jnp.float32)

    counts = [chunks, chunks * (chips - 1), chunks * (chips - 1), chunks * depth, chunks, 2, 2 * (chips - 1), 2 * (depth - 1)]
    one_round = [
        pltpu.VMEM((chips, width, 2 * terms), jnp.bfloat16),
        floats(chunks, depth, BLOCK, terms),
        floats(chunks, depth, BLOCK, terms),
        floats(chunks, BLOCK, terms),
        floats(total, BLOCK),
        floats(half, BLOCK),
        floats(chips - 1, piece, BLOCK),
        floats(depth - 1, portion, BLOCK),
        floats(total, BLOCK),
    ] + [pltpu.SemaphoreType.DMA((count,)) for count in counts for _ in range(2)]
    return pl.pallas_call(
        functools.partial(iterate_kernel, chips, depth),
        out_shape=jax.ShapeDtypeStruct((width, terms), jnp.float32),
        in_specs=[VMEM] * 3,
        out_specs=VMEM,
        scratch_shapes=[floats(width, terms), floats(width, width + terms), floats(BLOCK, 2 * BLOCK)] + one_round * ITERS,
        compiler_params=pltpu.CompilerParams(
            collective_id=0, has_side_effects=True, vmem_limit_bytes=56 * 2**20
        ),
    )(current, high, low)


def local(basis, tile_counts, tile_rows, tile_cols, tile_live, marginals):
    terms_here = basis.shape[1]
    row_count = lax.axis_size("rows")
    col_count = lax.axis_size("cols")
    row_index = lax.axis_index("rows")
    col_index = lax.axis_index("cols")
    group_size = row_count * terms_here
    marg_float = marginals.astype(jnp.float32)
    log_total = jnp.log(jnp.sum(marg_float)).reshape(1)
    log_margins = jnp.log(marg_float)
    row_logs = lax.dynamic_index_in_dim(
        log_margins.reshape(col_count, row_count, terms_here), row_index, 1, keepdims=False
    ).reshape(-1, 1)
    col_logs = lax.dynamic_slice_in_dim(log_margins, col_index * group_size, group_size).reshape(1, -1)
    high, low = build_matrix(tile_rows, tile_cols, tile_live, log_total, tile_counts, row_logs, col_logs)
    return iterate(basis, high, low)


def solution(mesh):
    in_specs = (
        P(None, ("cols", "rows")),
        P(("rows", "cols"), None, None),
        P(("rows", "cols")),
        P(("rows", "cols")),
        P(("rows", "cols")),
        P(),
    )
    out_specs = P(None, ("cols", "rows"))
    return jax.shard_map(local, mesh=mesh, in_specs=in_specs, out_specs=out_specs, check_vma=False)
```

profile of v0, /device:TPU:0, one launch (start us, length us, event | category | flops | bytes accessed | tf_op | source)
XLA Modules:
  0.0 158.4 jit_solution(10959747518198706955)
XLA Ops:
  0.7 1.3 convert_log_fusion
  2.7 0.6 dynamic_slice.8
  3.3 0.9 copy.7.row_logs_ref
  4.1 4.9 %shard_map.64 = (bf16[512,1024]{1,0:T(8,128)(2,1)}, bf16[512,1024]{1,0:T(8,128)(2,1)}) custom-call(s32[32]{0:T(128)} %rows_ref.1, s32[32]{0:T(128)} %cols_ref.1, s32[1]{0:T(128)S(6)} %copy.9.live_ref, f32[1]{0:T(128)} %bitcast.total_ref, s32[32,128,128]{2,1,0:T(8,128)} %counts_ref.1, f32[512,1]{1,0:T(8,128)} %copy.7.row_logs_ref, f32[1,1024]{1,0:T(1,128)} %bitcast.6), custom_call_target="tpu_custom_call" | custom-call | tf_op jit(solution)/shard_map/pallas_call | solution.py:70
  9.1 147.7 %shard_map.65 = f32[512,128]{1,0:T(8,128)} custom-call(f32[512,128]{1,0:T(8,128)} %cur_ref.1, bf16[512,1024]{1,0:T(8,128)(2,1)} %get-tuple-element.7.high_ref, bf16[512,1024]{1,0:T(8,128)(2,1)} %get-tuple-element.8.low_ref), custom_call_target="tpu_custom_call" | custom-call | tf_op jit(solution)/shard_map/pallas_call | solution.py:406
  156.8 1.7 %copy.10 = f32[512,128]{1,0:T(8,128)} copy(f32[512,128]{1,0:T(8,128)} %shard_map.65) | data formatting | bytes 524288
  (1 shorter events, 0.0 us)
where the time goes:
time: 159 us; the launch traced here: 158 us
  Pallas kernels  153 us (96%)
  local copies, waits for them, and re-layouts  3.14 us (2%)
    pallas_call x1, Pallas kernels, iterate(): pl.pallas_call(functools.partial(iterate_kernel, chips, depth), out_shape...  148 us
    pallas_call x1, Pallas kernels, build_matrix(): pl.pallas_call(matrix_kernel, out_shape=[jax.ShapeDtypeStruct(shape, jnp....  4.93 us

commit v1 on v0

--- a/solution.py
+++ b/solution.py
@@ -163,10 +163,12 @@
                 far_copy(q, k).start()
             near_copy(q).start()
 
-        def multiply(q):
+        def forward(q):
             for k in range(others):
                 far_copy(q, k).wait_recv()
                 pass_copy(q, k).start()
+
+        def multiply(q):
             near_copy(q).wait_recv()
             total = None
             for k in range(chips):
@@ -175,10 +177,10 @@
                 source = lax.rem(chip + chips - k, chips)
                 columns = pl.ds(pl.multiple_of(source * pair, pair), pair)
                 vectors = basis[source, block_at(q), :]
-                product = dot_nt(vectors, high_ref[:, columns], None) + dot_nt(vectors, low_ref[:, columns], None)
+                product = dot_nt(high_ref[:, columns], vectors, None) + dot_nt(low_ref[:, columns], vectors, None)
                 total = product if total is None else total + product
             for l in range(depth):
-                part[q, l] = total[:, l * terms : (l + 1) * terms]
+                part[q, l] = total[l * terms : (l + 1) * terms, :]
 
             @pl.when(level == 0)
             def _():
@@ -218,6 +220,8 @@
                 def _():
                     remote(part.at[q, u], inbox.at[q, u], sum_send.at[q * depth], sum_recv.at[q * depth + u], above).wait_recv()
                     share[block_at(q), :] += inbox[q, u]
+
+            share[block_at(q), :] = share[block_at(q), :].T
 
         def wait_sent(q):
             near_copy(q).wait_send()
@@ -300,7 +304,7 @@
                 work[i * BLOCK : (i + 1) * BLOCK, j * BLOCK : (j + 1) * BLOCK] = gram[index * BLOCK : (index + 1) * BLOCK, :]
             work[:, width:] = share[...]
 
-        return gather, multiply, pass_relay, collect, reduce_gram
+        return gather, forward, multiply, pass_relay, collect, reduce_gram
 
     sublane = lax.broadcasted_iota(jnp.int32, (PANEL, BLOCK), 0)
     unit = (
@@ -346,19 +350,32 @@
     per = len(rounds) // ITERS
     parts = [make_round(*rounds[it * per : (it + 1) * per]) for it in range(ITERS)]
     pl.semaphore_wait(barrier, len(peers))
-    gather, multiply = parts[0][:2]
+    gather, forward, multiply = parts[0][:3]
     each(chunks, lambda q: gather(q, cur_ref[block_at(q), :]))
-    each(chunks, multiply)
+    forward(0)
+
+    def first_step(q):
+        forward(q + 1)
+        multiply(q)
+
+    each(chunks - 1, first_step)
+    multiply(chunks - 1)
     for it in range(ITERS):
-        pass_relay, collect, reduce_gram = parts[it][2:]
+        pass_relay, collect, reduce_gram = parts[it][3:]
         each(chunks, pass_relay)
         each(chunks, collect)
         reduce_gram()
         if it + 1 < ITERS:
-            gather, multiply = parts[it + 1][:2]
+            gather, forward, multiply = parts[it + 1][:3]
 
             def step(b):
-                gather(b, eliminate(b))
+                solved = eliminate(b)
+                gather(b, solved)
+
+                @pl.when(b > 0)
+                def _():
+                    forward(b - 1)
+
                 update(b)
 
                 @pl.when(b > 0)
@@ -366,6 +383,7 @@
                     multiply(b - 1)
 
             each(chunks, step)
+            forward(chunks - 1)
             multiply(chunks - 1)
         else:
 

time: 159 us -> 161 us (1.013)
  Pallas kernels: 153 us -> 155 us
where the time goes in v1:
time: 161 us
  Pallas kernels  155 us (96%)
  local copies, waits for them, and re-layouts  3.14 us (2%)
    pallas_call x1, Pallas kernels, iterate(): pl.pallas_call(functools.partial(iterate_kernel, chips, depth), out_shape...  149 us
    pallas_call x1, Pallas kernels, build_matrix(): pl.pallas_call(matrix_kernel, out_shape=[jax.ShapeDtypeStruct(shape, jnp....  5.59 us

profile of v1, /device:TPU:0, one launch (start us, length us, event | category | flops | bytes accessed | tf_op | source)
XLA Modules:
  0.0 160.6 jit_solution(14876195207131639380)
XLA Ops:
  0.7 1.3 convert_log_fusion
  2.7 0.6 dynamic_slice.8
  3.3 0.9 copy.7.row_logs_ref
  4.1 5.6 %shard_map.64 = (bf16[512,1024]{1,0:T(8,128)(2,1)}, bf16[512,1024]{1,0:T(8,128)(2,1)}) custom-call(s32[32]{0:T(128)} %rows_ref.1, s32[32]{0:T(128)} %cols_ref.1, s32[1]{0:T(128)S(6)} %copy.9.live_ref, f32[1]{0:T(128)} %bitcast.total_ref, s32[32,128,128]{2,1,0:T(8,128)} %counts_ref.1, f32[512,1]{1,0:T(8,128)} %copy.7.row_logs_ref, f32[1,1024]{1,0:T(1,128)} %bitcast.6), custom_call_target="tpu_custom_call" | custom-call | tf_op jit(solution)/shard_map/pallas_call | solution.py:70
  9.7 149.1 %shard_map.65 = f32[512,128]{1,0:T(8,128)} custom-call(f32[512,128]{1,0:T(8,128)} %cur_ref.1, bf16[512,1024]{1,0:T(8,128)(2,1)} %get-tuple-element.7.high_ref, bf16[512,1024]{1,0:T(8,128)(2,1)} %get-tuple-element.8.low_ref), custom_call_target="tpu_custom_call" | custom-call | tf_op jit(solution)/shard_map/pallas_call | solution.py:424
  158.9 1.7 %copy.10 = f32[512,128]{1,0:T(8,128)} copy(f32[512,128]{1,0:T(8,128)} %shard_map.65) | data formatting | bytes 524288
  (1 shorter events, 0.0 us)

commit v2 on v1

--- a/solution.py
+++ b/solution.py
@@ -258,7 +258,6 @@
 
             half_start = core * half
             first = send(mine.at[rows_at((1 - core) * half, half)], core_in, core_send, core_recv, 0, sibling)
-            each(chunks, wait_sent)
             first.wait()
             mine[rows_at(half_start, half), :] += core_in[...]
 
@@ -267,6 +266,7 @@
                 send(mine.at[rows_at(half_start + lax.rem(chip + k, chips) * piece, piece)], plane_in.at[k - 1], plane_send, plane_recv, k - 1, plane[k - 1])
                 for k in range(1, chips)
             ]
+            each(chunks // 2, wait_sent)
             for copy in copies:
                 copy.wait()
             summed = mine[rows_at(piece_start, piece), :]
@@ -279,6 +279,7 @@
                 send(mine.at[rows_at(piece_start + lax.rem(level + k, depth) * portion, portion)], z_in.at[k - 1], z_send, z_recv, k - 1, column[k - 1])
                 for k in range(1, depth)
             ]
+            each(chunks - chunks // 2, lambda q: wait_sent(q + chunks // 2))
             for copy in copies:
                 copy.wait()
             summed = mine[rows_at(part_start, portion), :]
@@ -350,7 +351,7 @@
     per = len(rounds) // ITERS
     parts = [make_round(*rounds[it * per : (it + 1) * per]) for it in range(ITERS)]
     pl.semaphore_wait(barrier, len(peers))
-    gather, forward, multiply = parts[0][:3]
+    gather, forward, multiply, pass_relay = parts[0][:4]
     each(chunks, lambda q: gather(q, cur_ref[block_at(q), :]))
     forward(0)
 
@@ -358,15 +359,20 @@
         forward(q + 1)
         multiply(q)
 
+        @pl.when(q > 0)
+        def _():
+            pass_relay(q - 1)
+
     each(chunks - 1, first_step)
     multiply(chunks - 1)
+    pass_relay(chunks - 2)
+    pass_relay(chunks - 1)
     for it in range(ITERS):
-        pass_relay, collect, reduce_gram = parts[it][3:]
-        each(chunks, pass_relay)
+        collect, reduce_gram = parts[it][4:]
         each(chunks, collect)
         reduce_gram()
         if it + 1 < ITERS:
-            gather, forward, multiply = parts[it + 1][:3]
+            gather, forward, multiply, pass_relay = parts[it + 1][:4]
 
             def step(b):
                 solved = eliminate(b)
@@ -382,9 +388,15 @@
                 def _():
                     multiply(b - 1)
 
+                @pl.when(b > 1)
+                def _():
+                    pass_relay(b - 2)
+
             each(chunks, step)
             forward(chunks - 1)
+            pass_relay(chunks - 2)
             multiply(chunks - 1)
+            pass_relay(chunks - 1)
         else:
 
             def final(b):

time: 161 us -> 159 us (0.988)
  Pallas kernels: 155 us -> 152 us
where the time goes in v2:
time: 159 us; the launch traced here: 158 us
  Pallas kernels  152 us (96%)
  local copies, waits for them, and re-layouts  3.14 us (2%)
    pallas_call x1, Pallas kernels, iterate(): pl.pallas_call(functools.partial(iterate_kernel, chips, depth), out_shape...  148 us
    pallas_call x1, Pallas kernels, build_matrix(): pl.pallas_call(matrix_kernel, out_shape=[jax.ShapeDtypeStruct(shape, jnp....  4.37 us

profile of v2, /device:TPU:0, one launch (start us, length us, event | category | flops | bytes accessed | tf_op | source)
XLA Modules:
  0.0 158.3 jit_solution(6904457809534381528)
XLA Ops:
  0.7 1.3 convert_log_fusion
  2.7 0.6 dynamic_slice.8
  3.3 0.9 copy.7.row_logs_ref
  4.1 4.4 %shard_map.64 = (bf16[512,1024]{1,0:T(8,128)(2,1)}, bf16[512,1024]{1,0:T(8,128)(2,1)}) custom-call(s32[32]{0:T(128)} %rows_ref.1, s32[32]{0:T(128)} %cols_ref.1, s32[1]{0:T(128)S(6)} %copy.9.live_ref, f32[1]{0:T(128)} %bitcast.total_ref, s32[32,128,128]{2,1,0:T(8,128)} %counts_ref.1, f32[512,1]{1,0:T(8,128)} %copy.7.row_logs_ref, f32[1,1024]{1,0:T(1,128)} %bitcast.6), custom_call_target="tpu_custom_call" | custom-call | tf_op jit(solution)/shard_map/pallas_call | solution.py:70
  8.5 148.1 %shard_map.65 = f32[512,128]{1,0:T(8,128)} custom-call(f32[512,128]{1,0:T(8,128)} %cur_ref.1, bf16[512,1024]{1,0:T(8,128)(2,1)} %get-tuple-element.7.high_ref, bf16[512,1024]{1,0:T(8,128)(2,1)} %get-tuple-element.8.low_ref), custom_call_target="tpu_custom_call" | custom-call | tf_op jit(solution)/shard_map/pallas_call | solution.py:436
  156.6 1.7 %copy.10 = f32[512,128]{1,0:T(8,128)} copy(f32[512,128]{1,0:T(8,128)} %shard_map.65) | data formatting | bytes 524288
  (1 shorter events, 0.0 us)
